TPU v7x, 32 devices: a whole 2x2x4 slice. The times are simulated.
32 devices in a mesh: group: 2 (over y), freq: 4 (over z), support: 2 (over x), row: 2 (over core).
Axes of the slice: x: 2, y: 2, z: 4, core: 2. Of those that a mesh axis runs over, the one named last changes fastest.
Arguments:
- coherency: bfloat16 [4, 2048, 2048], P('freq', ('support', 'row')), as said below
- phases: int32 [4, 2048, 64], P('freq', ('support', 'row'), 'group'), parts along dimension 2, may hold values from 0 to 63
- influence: bfloat16 [2048, 2048], P(('support', 'row')), may hold values from -0.1875 to 0.1875
- mode_freq: float32 [2048], replicated, may hold values from 1 to 3
- damping: float32 [2048], replicated, may hold values from 0.3 to 0.7
- shapes: bfloat16 [2048, 2048], P(None, ('support', 'row')), may hold values from -0.1875 to 0.1875
Outputs:
- displacement: float32 [8, 64, 2048], P(None, ('group', 'freq'), ('support', 'row')), parts along dimension 1
There are 2 independent parts, one for each index of `group`. A program takes and returns all parts, laid end to end along the dimension named above; an argument that names none is the same for every part. Nothing has to cross between parts.
Inputs may be any that keep to these rules, and one draw needn't show every extreme that they name: coherency[f] is lower triangular, with a positive diagonal between 0.8 and 1.5 that is the largest entry of each row.
All inputs are finite; a program needn't handle non-finite values.
Results may differ from a plain program's by a relative error of at most 0.018.
Values may be sent and summed in bfloat16 or wider, within the bound.
A program may use at most 64 MiB of HBM per device.

v0:
```python
import math

import jax
import jax.numpy as jnp
from jax import lax
from jax.sharding import PartitionSpec as P

NPH = 64


def body(coherency, phases, influence, mode_freq, damping, shapes):
    freq_local = phases.shape[0]
    real_grand_total = phases.shape[2]
    mode_total = influence.shape[1]
    block_count = lax.axis_size(("support", "row"))
    mode_local = mode_total // block_count
    freq_total = freq_local * lax.axis_size("freq")
    time_total = 2 * freq_total
    angle = phases.astype(jnp.float32) * (2.0 * math.pi / NPH)
    local_table = jnp.concatenate([jnp.cos(angle), jnp.sin(angle)], -1).astype(jnp.bfloat16)
    power_spectra = jnp.einsum(
        "dco,dou->dcu",
        coherency,
        lax.all_gather(local_table, ("support", "row"), axis=1, tiled=True),
        preferred_element_type=jnp.float32,
    )
    power_spectra = power_spectra.astype(jnp.bfloat16)
    my_block = lax.axis_index(("support", "row"))
    single_term = jnp.einsum(
        "xh,axe->hae", influence, power_spectra, preferred_element_type=jnp.float32
    )
    summed_result = lax.psum(single_term.astype(jnp.bfloat16), ("support", "row")).astype(
        jnp.float32
    )
    own_forces = lax.dynamic_slice_in_dim(summed_result, my_block * mode_local, mode_local, 0)
    own_freq = lax.dynamic_slice_in_dim(mode_freq, my_block * mode_local, mode_local, 0)
    local_damping_ratio = lax.dynamic_slice_in_dim(damping, my_block * mode_local, mode_local, 0)
    freq_first = lax.axis_index("freq") * freq_local
    omega = ((freq_first + jnp.arange(freq_local) + 1).astype(jnp.float32) * (2.5 / freq_total))[
        None, :
    ]
    mode_sq = (own_freq * own_freq)[:, None]
    real_den = mode_sq - omega * omega
    imag_den = 2.0 * local_damping_ratio[:, None] * own_freq[:, None] * omega
    denom = real_den * real_den + imag_den * imag_den
    recep_re = (mode_sq * real_den / denom)[:, :, None]
    recep_im = (-mode_sq * imag_den / denom)[:, :, None]
    force_re = own_forces[:, :, :real_grand_total]
    force_imaginary = own_forces[:, :, real_grand_total:]
    resp_re = recep_re * force_re - recep_im * force_imaginary
    resp_im = recep_re * force_imaginary + recep_im * force_re
    response = jnp.transpose(jnp.stack([resp_re, resp_im], 0), (2, 0, 3, 1))
    steps_n = jnp.arange(time_total)
    bins = jnp.arange(freq_total) + 1
    wrapped = steps_n[:, None] * bins[None, :] % time_total
    theta = wrapped.astype(jnp.float32) * (2.0 * math.pi / time_total)
    factor_scale = jnp.float32(math.sqrt(2.0 / freq_total))
    inverse_table = jnp.stack([jnp.cos(theta) * factor_scale, -jnp.sin(theta) * factor_scale], -1)
    modal = jnp.einsum(
        "nfc,fcrm->nrm",
        inverse_table,
        lax.all_to_all(
            response.astype(jnp.bfloat16), "freq", split_axis=2, concat_axis=0, tiled=True
        ).astype(response.dtype),
        precision=lax.Precision.HIGHEST,
    )
    real_local = modal.shape[1]
    modal_rows = modal.astype(jnp.bfloat16).reshape(time_total * real_local, mode_local)
    dof_local = shapes.shape[0] // block_count
    slab = lax.psum_scatter(
        lax.dot_general(
            shapes, modal_rows, (((1,), (1,)), ((), ())), preferred_element_type=jnp.float32
        ).astype(jnp.bfloat16),
        ("support", "row"),
        scatter_dimension=0,
        tiled=True,
    ).astype(jnp.float32)
    return jnp.transpose(slab).reshape(time_total, real_local, dof_local)


def solution(mesh):
    return jax.shard_map(
        body,
        mesh=mesh,
        in_specs=(
            P("freq", ("support", "row"), None),
            P("freq", ("support", "row"), "group"),
            P(("support", "row"), None),
            P(),
            P(),
            P(None, ("support", "row")),
        ),
        out_specs=P(None, ("group", "freq"), ("support", "row")),
        check_vma=False,
    )
```

profile of v0, /device:TPU:1, one launch (start us, length us, event | category | flops | bytes accessed | tf_op | source)
XLA Modules:
  0.0 92.7 jit_solution(14076296209351996642)
XLA Ops:
  6.5 0.0 copy-start
  6.5 0.0 all-reduce.2.cloned.1.call-start
  6.5 1.2 %cosine_convert_fusion = (bf16[1,512,32]{1,2,0:T(8,128)(2,1)S(1)}, bf16[1,512,32]{1,2,0:T(8,128)(2,1)S(1)}) fusion(s32[1,512,32]{1,2,0:T(8,128)} %param.7), kind=kLoop, calls=%fused_computation.21 | loop fusion | flops 65536 | bytes 131072 | tf_op jit(solution)/shard_map/convert.6
  7.8 7.1 %all_gather.3 = bf16[1,2048,64]{1,2,0:T(8,128)(2,1)S(1)} all-gather(bf16[1,512,64]{1,2,0:T(8,128)(2,1)S(1)} %pad_maximum_fusion), channel_id=1, replica_groups=mesh['group'=2,'freq'=4,'support'=2,'row'=2] {'support','row'}, dimensions={1}, use_global_device_ids=true | all-gather | bytes 327680 | tf_op jit(solution)/shard_map/all_gather | solution.py:24
  14.9 0.0 copy-done
  14.9 3.5 %fusion = bf16[2048,1,64]{0,2,1:T(8,128)(2,1)} fusion(bf16[512,2048]{1,0:T(8,128)(2,1)S(1)} %copy-done, bf16[1,512,2048]{2,1,0:T(8,128)(2,1)} %param.6, bf16[1,2048,64]{1,2,0:T(8,128)(2,1)S(1)} %all_gather.3), kind=kOutput, calls=%fused_computation.2 | convolution fusion | flops 268599296 | bytes 4718592 | tf_op jit(solution)/shard_map/xh,axe->hae/dot_general | solution.py:29
  18.4 0.0 all-reduce.2.cloned.1.call-update
  18.4 0.8 fusion.20
  19.2 30.6 %all-reduce.2.cloned.1.call-done = bf16[2048,1,64]{0,2,1:T(8,128)(2,1)} async-done(((bf16[2048,1,64]{0,2,1:T(8,128)(2,1)}), bf16[2048,1,64]{0,2,1:T(8,128)(2,1)}) %all-reduce.2.cloned.1.call-update) | async-done | bytes 262160 | tf_op jit(solution)/shard_map/psum | solution.py:32
  49.8 0.8 dynamic-slice_convert_fusion
  50.7 0.7 copy.16
  51.4 4.7 %all-to-all-start = ((bf16[1,2,32,512]{3,1,0,2:T(2,128)(2,1)}), bf16[1,2,32,512]{3,1,0,2:T(2,128)(2,1)S(1)}, u32[]{:S(2)}, u32[]{:S(2)}) async-start(bf16[1,2,32,512]{3,1,0,2:T(2,128)(2,1)} %copy.16), calls=%async_computation | async-start | bytes 131072 | tf_op jit(solution)/shard_map/all_to_all | solution.py:62
  56.1 0.0 reduce-scatter.2.cloned.1.call-start
  56.1 0.1 cosine_multiply_fusion
  56.2 4.5 %all-to-all-done = bf16[1,2,32,512]{3,1,0,2:T(2,128)(2,1)S(1)} async-done(((bf16[1,2,32,512]{3,1,0,2:T(2,128)(2,1)}), bf16[1,2,32,512]{3,1,0,2:T(2,128)(2,1)S(1)}, u32[]{:S(2)}, u32[]{:S(2)}) %all-to-all-start) | async-done | bytes 65568 | tf_op jit(solution)/shard_map/all_to_all | solution.py:62
  60.7 0.3 fusion.4
  61.0 3.0 %fusion.1 = bf16[2048,64]{0,1:T(8,128)(2,1)} fusion(bf16[2048,512]{1,0:T(8,128)(2,1)} %param.11, bf16[8,8,512]{2,0,1:T(8,128)(2,1)S(1)} %fusion.4), kind=kOutput, calls=%fused_computation.3 | convolution fusion | flops 134348800 | bytes 2424832 | tf_op jit(solution)/shard_map/dot_general | solution.py:71
  64.0 0.0 reduce-scatter.2.cloned.1.call-update
  64.0 20.3 %reduce-scatter.2.cloned.1.call-done = bf16[512,64]{0,1:T(8,128)(2,1)} async-done(((bf16[2048,64]{0,1:T(8,128)(2,1)}), bf16[512,64]{0,1:T(8,128)(2,1)}) %reduce-scatter.2.cloned.1.call-update) | async-done | bytes 65552 | tf_op jit(solution)/shard_map/reduce_scatter | solution.py:70
  84.3 1.5 %convert_bitcast_fusion = f32[8,8,512]{2,1,0:T(8,128)} fusion(bf16[512,64]{0,1:T(8,128)(2,1)} %reduce-scatter.2.cloned.1.call-done), kind=kLoop, calls=%fused_computation.10 | loop fusion | flops 32768 | bytes 196608 | tf_op jit(solution)/shard_map/reshape | solution.py:78
  (4 shorter events, 0.0 us)
Async XLA Ops:
  6.5 8.3 %copy-start = (bf16[512,2048]{1,0:T(8,128)(2,1)S(1)}, bf16[512,2048]{1,0:T(8,128)(2,1)}, u32[]{:S(2)}) copy-start(bf16[512,2048]{1,0:T(8,128)(2,1)} %param.8) | copy-start | bytes 6291460
  6.5 43.3 %all-reduce.2.cloned.1.call-start = ((), (), s32[]{:S(2)}) async-start(), calls=%async_computation.2 | async-start | bytes 524288 | tf_op jit(solution)/shard_map/psum | solution.py:32
  51.4 9.3 %all-to-all-start = ((bf16[1,2,32,512]{3,1,0,2:T(2,128)(2,1)}), bf16[1,2,32,512]{3,1,0,2:T(2,128)(2,1)S(1)}, u32[]{:S(2)}, u32[]{:S(2)}) async-start(bf16[1,2,32,512]{3,1,0,2:T(2,128)(2,1)} %copy.16), calls=%async_computation | async-start | bytes 131072 | tf_op jit(solution)/shard_map/all_to_all | solution.py:62
  56.1 28.2 %reduce-scatter.2.cloned.1.call-start = ((), (), s32[]{:S(2)}) async-start(), calls=%async_computation.3 | async-start | bytes 327680 | tf_op jit(solution)/shard_map/reduce_scatter | solution.py:70
Sparse Core Ops, SparseCore 0:
  18.5 31.2 all-reduce.1
  64.2 20.1 reduce-scatter.1
where the time goes:
time: 93.8 us; the launch traced here: 92.7 us
  waiting for transfers between devices  55.4 us (59%)
  between operations  13.4 us (14%)
  blocking collectives  7.09 us (8%)
  matrix products  6.81 us (7%)
  starting transfers between devices  4.7 us (5%)
  other arithmetic  4.53 us (5%)
    psum x1, waiting for transfers between devices, body(): lax.psum(single_term.astype(jnp.bfloat16), ('support', 'row'))  30.6 us
    reduce_scatter x1, waiting for transfers between devices, body(): lax.psum_scatter(lax.dot_general(shapes, modal_rows, (((1,), (1,)), ((),...  20.3 us
    all_gather x1, blocking collectives, body(): lax.all_gather(local_table, ('support', 'row'), axis=1, tiled=True)  7.09 us
    all_to_all x1, starting transfers between devices, body(): lax.all_to_all(response.astype(jnp.bfloat16), 'freq', split_axis=2, conca...  4.7 us
    all_to_all x1, waiting for transfers between devices, body(): lax.all_to_all(response.astype(jnp.bfloat16), 'freq', split_axis=2, conca...  4.47 us
    dot_general x1, matrix products, body(): jnp.einsum('xh,axe->hae', influence, power_spectra, preferred_element_typ...  3.48 us
    dot_general x1, matrix products, body(): lax.dot_general(shapes, modal_rows, (((1,), (1,)), ((), ())), preferred_e...  3.05 us
  transfers between devices with their start and end apart: 3, of which 3 were waited for; matrix products, arithmetic and copies ran while one was open for 1% of the time, Pallas kernels for 0%

commit v1 on v0

v1 whole, which is shorter than its diff:
```python
import functools
import math

import jax
import jax.numpy as jnp
import numpy as np
from jax import lax
from jax.experimental import pallas as pl
from jax.experimental.pallas import tpu as pltpu
from jax.sharding import PartitionSpec as P

NPH = 64
MESH = pl.DeviceIdType.MESH
NT = (((1,), (1,)), ((), ()))
NN = (((1,), (0,)), ((), ()))


def cos_sin(phase):
    quarter = NPH // 4
    quadrant = (phase + quarter // 2) // quarter
    x = (phase - quadrant * quarter).astype(jnp.float32) * (2.0 * math.pi / NPH)
    quadrant = quadrant % 4
    y = x * x
    c = 1.0 + y * (-0.5 + y * (1 / 24 + y * (-1 / 720 + y * (1 / 40320 - y * (1 / 3628800)))))
    s = x * (1.0 + y * (-1 / 6 + y * (1 / 120 + y * (-1 / 5040 + y * (1 / 362880)))))
    odd = (quadrant == 1) | (quadrant == 3)
    cos = jnp.where(odd, s, c)
    sin = jnp.where(odd, c, s)
    cos = jnp.where((quadrant == 1) | (quadrant == 2), -cos, cos)
    sin = jnp.where(quadrant >= 2, -sin, sin)
    return cos, sin


def time_factors(freq_total):
    time_total = 2 * freq_total
    wrapped = np.arange(time_total)[:, None] * (np.arange(freq_total) + 1)[None, :] % time_total
    theta = wrapped * (2.0 * math.pi / time_total)
    scale = math.sqrt(2.0 / freq_total)
    return np.cos(theta) * scale, -np.sin(theta) * scale


def kernel(
    n_support, n_row, n_freq,
    coh_in, ph_in, infl_in, mf_in, dp_in, shp_in,
    out_ref,
    coh, ph, infl, mf, dp, shp,
    tab, f_send, f_recv, r_send, r_recv, d_send, d_recv,
    local_sem, a_out, a_in, b_out, b_in, c_out, c_in, d_out, d_in,
):
    blocks = n_support * n_row
    real = ph.shape[0]
    depth = ph.shape[1]
    modes = shp.shape[1]
    real_local = real // n_freq
    dofs = shp.shape[0] // blocks
    my_support, my_row = lax.axis_index("support"), lax.axis_index("row")
    my_freq = lax.axis_index("freq")
    mine = my_support * n_row + my_row

    locals_ = [
        pltpu.make_async_copy(src, dst, local_sem.at[i])
        for i, (src, dst) in enumerate(
            [(ph_in, ph), (mf_in, mf), (dp_in, dp), (coh_in.at[0], coh), (infl_in, infl), (shp_in, shp)]
        )
    ]
    for copy in locals_:
        copy.start()

    def to_block(k):
        return {
            "support": lax.rem(my_support + k // n_row, n_support),
            "row": lax.rem(my_row + k % n_row, n_row),
        }

    def block_to(k):
        at = to_block(k)
        return at["support"] * n_row + at["row"]

    def block_from(k):
        s = lax.rem(my_support + n_support - k // n_row, n_support)
        r = lax.rem(my_row + n_row - k % n_row, n_row)
        return s * n_row + r

    def to_freq(k):
        return {"freq": lax.rem(my_freq + k, n_freq)}

    barrier = pltpu.get_barrier_semaphore()
    for k in range(1, blocks):
        pl.semaphore_signal(barrier, inc=1, device_id=to_block(k), device_id_type=MESH)
    for k in range(1, n_freq):
        pl.semaphore_signal(barrier, inc=1, device_id=to_freq(k), device_id_type=MESH)

    far_first = [k for k in range(1, blocks) if k >= n_row] + [k for k in range(1, blocks) if k < n_row]
    near_first = [k for k in range(1, blocks)]

    locals_[0].wait()
    cos, sin = cos_sin(ph[...])
    tab[0] = jnp.concatenate([cos, sin], 0).astype(jnp.bfloat16)

    pl.semaphore_wait(barrier, blocks - 1 + n_freq - 1)

    def send(src, dst, out_sem, in_sem, target):
        copy = pltpu.make_async_remote_copy(
            src_ref=src, dst_ref=dst, send_sem=out_sem, recv_sem=in_sem,
            device_id=target, device_id_type=MESH,
        )
        copy.start()
        return copy

    a_copies = {
        k: send(tab.at[0], tab.at[k], a_out.at[k], a_in.at[k], to_block(k)) for k in far_first
    }

    locals_[1].wait()
    locals_[2].wait()
    my_modes = pl.ds(pl.multiple_of(mine * modes, modes), modes)
    freq = mf[:, my_modes]
    omega = (my_freq + 1).astype(jnp.float32) * (2.5 / n_freq)
    mode_sq = freq * freq
    real_den = mode_sq - omega * omega
    imag_den = 2.0 * dp[:, my_modes] * freq * omega
    denom = real_den * real_den + imag_den * imag_den
    recep_re = mode_sq * real_den / denom
    recep_im = -mode_sq * imag_den / denom

    def spectra_term(k):
        columns = pl.ds(pl.multiple_of(block_from(k) * depth, depth), depth)
        return lax.dot_general(tab[k], coh[:, columns], NT, preferred_element_type=jnp.float32)

    locals_[3].wait()
    spectra = spectra_term(0)
    for k in near_first:
        a_copies[k].wait_recv()
        spectra += spectra_term(k)
    spectra = spectra.astype(jnp.bfloat16)

    def force_term(k):
        columns = pl.ds(pl.multiple_of(block_to(k) * modes, modes), modes)
        return lax.dot_general(
            spectra, infl[:, columns], NN, preferred_element_type=jnp.float32
        ).astype(jnp.bfloat16)

    locals_[4].wait()
    b_copies = {}
    for k in far_first:
        f_send[k] = force_term(k)
        b_copies[k] = send(f_send.at[k], f_recv.at[k], b_out.at[k], b_in.at[k], to_block(k))
    forces = force_term(0).astype(jnp.float32)
    for k in near_first:
        b_copies[k].wait_recv()
        forces += f_recv[k].astype(jnp.float32)

    force_re, force_im = forces[:real], forces[real:]
    resp_re = recep_re * force_re - recep_im * force_im
    resp_im = recep_re * force_im + recep_im * force_re
    for f in range(n_freq):
        rows = slice(f * real_local, (f + 1) * real_local)
        r_send[f] = jnp.concatenate([resp_re[rows], resp_im[rows]], 0).astype(jnp.bfloat16)
    c_copies = {
        k: send(
            r_send.at[lax.rem(my_freq + k, n_freq)], r_recv.at[my_freq],
            c_out.at[k], c_in.at[k], to_freq(k),
        )
        for k in range(1, n_freq)
    }
    r_recv[my_freq] = r_send[my_freq]
    for k in range(1, n_freq):
        c_copies[k].wait_recv()

    cos_table, sin_table = time_factors(n_freq)
    parts = [r_recv[f].astype(jnp.float32) for f in range(n_freq)]
    rows = []
    for n in range(2 * n_freq):
        total = None
        for f in range(n_freq):
            term = parts[f][:real_local] * float(cos_table[n, f])
            term += parts[f][real_local:] * float(sin_table[n, f])
            total = term if total is None else total + term
        rows.append(total)
    modal = jnp.concatenate(rows, 0).astype(jnp.bfloat16)

    def slab_term(k):
        block_rows = pl.ds(pl.multiple_of(block_to(k) * dofs, dofs), dofs)
        return lax.dot_general(
            modal, shp[block_rows, :], NT, preferred_element_type=jnp.float32
        ).astype(jnp.bfloat16)

    locals_[5].wait()
    d_copies = {}
    for k in far_first:
        d_send[k] = slab_term(k)
        d_copies[k] = send(d_send.at[k], d_recv.at[k], d_out.at[k], d_in.at[k], to_block(k))
    slab = slab_term(0).astype(jnp.float32)
    for k in near_first:
        d_copies[k].wait_recv()
        slab += d_recv[k].astype(jnp.float32)
    out_ref[...] = slab

    for copies in (a_copies, b_copies, c_copies, d_copies):
        for copy in copies.values():
            copy.wait_send()


def body(coherency, phases, influence, mode_freq, damping, shapes):
    n_support, n_row = lax.axis_size("support"), lax.axis_size("row")
    n_freq = lax.axis_size("freq")
    blocks = n_support * n_row
    depth, real = phases.shape[1], phases.shape[2]
    mode_total, modes = influence.shape[1], shapes.shape[1]
    dofs = shapes.shape[0] // blocks
    real_local = real // n_freq
    times = 2 * n_freq
    bf16, f32 = jnp.bfloat16, jnp.float32
    dma = pltpu.SemaphoreType.DMA
    slab = pl.pallas_call(
        functools.partial(kernel, n_support, n_row, n_freq),
        out_shape=jax.ShapeDtypeStruct((times * real_local, dofs), f32),
        in_specs=[pl.BlockSpec(memory_space=pltpu.HBM)] * 6,
        out_specs=pl.BlockSpec(memory_space=pltpu.VMEM),
        scratch_shapes=[
            pltpu.VMEM(coherency.shape[1:], bf16),
            pltpu.VMEM((real, depth), jnp.int32),
            pltpu.VMEM(influence.shape, bf16),
            pltpu.VMEM((1, mode_total), f32),
            pltpu.VMEM((1, mode_total), f32),
            pltpu.VMEM(shapes.shape, bf16),
            pltpu.VMEM((blocks, 2 * real, depth), bf16),
            pltpu.VMEM((blocks, 2 * real, modes), bf16),
            pltpu.VMEM((blocks, 2 * real, modes), bf16),
            pltpu.VMEM((n_freq, 2 * real_local, modes), bf16),
            pltpu.VMEM((n_freq, 2 * real_local, modes), bf16),
            pltpu.VMEM((blocks, times * real_local, dofs), bf16),
            pltpu.VMEM((blocks, times * real_local, dofs), bf16),
            dma((6,)),
            dma((blocks,)), dma((blocks,)),
            dma((blocks,)), dma((blocks,)),
            dma((n_freq,)), dma((n_freq,)),
            dma((blocks,)), dma((blocks,)),
        ],
        compiler_params=pltpu.CompilerParams(
            collective_id=0, has_side_effects=True, vmem_limit_bytes=60 * 1024 * 1024
        ),
    )(
        coherency,
        jnp.transpose(phases[0]),
        influence,
        mode_freq.reshape(1, mode_total),
        damping.reshape(1, mode_total),
        shapes,
    )
    return slab.reshape(times, real_local, dofs)


def solution(mesh):
    return jax.shard_map(
        body,
        mesh=mesh,
        in_specs=(
            P("freq", ("support", "row"), None),
            P("freq", ("support", "row"), "group"),
            P(("support", "row"), None),
            P(),
            P(),
            P(None, ("support", "row")),
        ),
        out_specs=P(None, ("group", "freq"), ("support", "row")),
        check_vma=False,
    )
```

time: 93.8 us -> 23.9 us (0.25); the launches traced: 92.7 us -> 23.8 us
  waiting for transfers between devices: 55.4 us -> 0 us
  Pallas kernels: 0 us -> 22.2 us
  between operations: 13.4 us -> 0.01 us
  blocking collectives: 7.09 us -> 0 us
  matrix products: 6.81 us -> 0 us
  starting transfers between devices: 4.7 us -> 0 us
  other arithmetic: 4.53 us -> 0 us
    psum x1 -> x0, waiting for transfers between devices: 30.6 us -> none  [body(): lax.psum(single_term.astype(jnp.bfloat16), ('support', 'row'))]
    pallas_call x0 -> x1, Pallas kernels: none -> 22.2 us  [body(): pl.pallas_call(functools.partial(kernel, n_support, n_row, n_freq), out_s...]
    reduce_scatter x1 -> x0, waiting for transfers between devices: 20.3 us -> none  [body(): lax.psum_scatter(lax.dot_general(shapes, modal_rows, (((1,), (1,)), ((),...]
    all_gather x1 -> x0, blocking collectives: 7.09 us -> none  [body(): lax.all_gather(local_table, ('support', 'row'), axis=1, tiled=True)]
    dot_general x3 -> x0, matrix products: 6.81 us -> none  [the longest x1 3.48 us: body(): jnp.einsum('xh,axe->hae', influence, power_spectra, preferred_element_typ...]
    all_to_all x1 -> x0, starting transfers between devices: 4.7 us -> none  [body(): lax.all_to_all(response.astype(jnp.bfloat16), 'freq', split_axis=2, conca...]
    all_to_all x1 -> x0, waiting for transfers between devices: 4.47 us -> none  [body(): lax.all_to_all(response.astype(jnp.bfloat16), 'freq', split_axis=2, conca...]
    unnamed x2 -> x1, local copies, waits for them, and re-layouts: 0.01 us -> 1.57 us
  transfers between devices with their start and end apart: 3 -> 0, of which waited for: 3 -> 0; matrix products, arithmetic and copies ran while one was open for 1% -> 0% of each run, Pallas kernels for 0% -> 0%
where the time goes in v1:
time: 23.9 us; the launch traced here: 23.8 us
  Pallas kernels  22.2 us (93%)
  local copies, waits for them, and re-layouts  1.57 us (7%)
    pallas_call x1, Pallas kernels, body(): pl.pallas_call(functools.partial(kernel, n_support, n_row, n_freq), out_s...  22.2 us
    unnamed x1, local copies, waits for them, and re-layouts  1.57 us

profile of v1, /device:TPU:1, one launch (start us, length us, event | category | flops | bytes accessed | tf_op | source)
XLA Modules:
  0.0 23.8 jit_solution(14609435764897019610)
XLA Ops:
  0.0 22.2 %shard_map.64 = f32[64,512]{1,0:T(8,128)} custom-call(bf16[1,512,2048]{2,1,0:T(8,128)(2,1)} %coh_in.1, s32[32,512]{1,0:T(8,128)} %bitcast.7, bf16[512,2048]{1,0:T(8,128)(2,1)} %infl_in.1, f32[1,2048]{1,0:T(1,128)} %bitcast.8, f32[1,2048]{1,0:T(1,128)} %bitcast.9, bf16[2048,512]{1,0:T(8,128)(2,1)} %shp_in.1), custom_call_target="tpu_custom_call" | custom-call | tf_op jit(solution)/shard_map/pallas_call | solution.py:215
  22.2 1.6 %copy.8 = f32[8,8,512]{2,1,0:T(8,128)} copy(f32[8,8,512]{2,1,0:T(8,128)} %bitcast.6) | data formatting | bytes 262144

commit v2 on v1

--- a/solution.py
+++ b/solution.py
@@ -10,6 +10,7 @@
 from jax.sharding import PartitionSpec as P
 
 NPH = 64
+PIECES = 2
 MESH = pl.DeviceIdType.MESH
 NT = (((1,), (1,)), ((), ()))
 NN = (((1,), (0,)), ((), ()))
@@ -107,9 +108,20 @@
         copy.start()
         return copy
 
-    a_copies = {
-        k: send(tab.at[0], tab.at[k], a_out.at[k], a_in.at[k], to_block(k)) for k in far_first
-    }
+    far = [k for k in far_first if k >= n_row]
+    near = [k for k in near_first if k < n_row]
+    rows = 2 * real // PIECES
+    pieces = [pl.ds(c * rows, rows) for c in range(PIECES)]
+
+    def send_piece(src, dst, k, c, out_sem, in_sem):
+        return send(
+            src.at[pieces[c]], dst.at[pieces[c]], out_sem.at[k, c], in_sem.at[k, c], to_block(k)
+        )
+
+    a_copies = {}
+    for c in range(PIECES):
+        for k in far + near:
+            a_copies[k, c] = send_piece(tab.at[0], tab.at[k], k, c, a_out, a_in)
 
     locals_[1].wait()
     locals_[2].wait()
@@ -123,32 +135,45 @@
     recep_re = mode_sq * real_den / denom
     recep_im = -mode_sq * imag_den / denom
 
-    def spectra_term(k):
+    def spectra_term(k, part):
         columns = pl.ds(pl.multiple_of(block_from(k) * depth, depth), depth)
-        return lax.dot_general(tab[k], coh[:, columns], NT, preferred_element_type=jnp.float32)
+        return lax.dot_general(
+            tab[k, part], coh[:, columns], NT, preferred_element_type=jnp.float32
+        )
 
     locals_[3].wait()
-    spectra = spectra_term(0)
-    for k in near_first:
-        a_copies[k].wait_recv()
-        spectra += spectra_term(k)
-    spectra = spectra.astype(jnp.bfloat16)
-
-    def force_term(k):
+    whole = pl.ds(0, 2 * real)
+    spectra_near = spectra_term(0, whole)
+    for k in near:
+        for c in range(PIECES):
+            a_copies[k, c].wait_recv()
+        spectra_near += spectra_term(k, whole)
+
+    def force_term(spectra, k):
         columns = pl.ds(pl.multiple_of(block_to(k) * modes, modes), modes)
         return lax.dot_general(
             spectra, infl[:, columns], NN, preferred_element_type=jnp.float32
         ).astype(jnp.bfloat16)
 
-    locals_[4].wait()
     b_copies = {}
-    for k in far_first:
-        f_send[k] = force_term(k)
-        b_copies[k] = send(f_send.at[k], f_recv.at[k], b_out.at[k], b_in.at[k], to_block(k))
-    forces = force_term(0).astype(jnp.float32)
-    for k in near_first:
-        b_copies[k].wait_recv()
-        forces += f_recv[k].astype(jnp.float32)
+    forces = []
+    for c in range(PIECES):
+        spectra = spectra_near[c * rows : (c + 1) * rows]
+        for k in far:
+            a_copies[k, c].wait_recv()
+            spectra += spectra_term(k, pieces[c])
+        spectra = spectra.astype(jnp.bfloat16)
+        if c == 0:
+            locals_[4].wait()
+        for k in far_first:
+            f_send[k, pieces[c]] = force_term(spectra, k)
+            b_copies[k, c] = send_piece(f_send.at[k], f_recv.at[k], k, c, b_out, b_in)
+        forces.append(force_term(spectra, 0).astype(jnp.float32))
+    for c in range(PIECES):
+        for k in near_first:
+            b_copies[k, c].wait_recv()
+            forces[c] += f_recv[k, pieces[c]].astype(jnp.float32)
+    forces = jnp.concatenate(forces, 0)
 
     force_re, force_im = forces[:real], forces[real:]
     resp_re = recep_re * force_re - recep_im * force_im
@@ -232,8 +257,8 @@
             pltpu.VMEM((blocks, times * real_local, dofs), bf16),
             pltpu.VMEM((blocks, times * real_local, dofs), bf16),
             dma((6,)),
-            dma((blocks,)), dma((blocks,)),
-            dma((blocks,)), dma((blocks,)),
+            dma((blocks, PIECES)), dma((blocks, PIECES)),
+            dma((blocks, PIECES)), dma((blocks, PIECES)),
             dma((n_freq,)), dma((n_freq,)),
             dma((blocks,)), dma((blocks,)),
         ],

time: 23.9 us -> 23.5 us (0.983)
  Pallas kernels: 22.2 us -> 21.8 us
    pallas_call x1, Pallas kernels: 22.2 us -> 21.8 us  [body(): pl.pallas_call(functools.partial(kernel, n_support, n_row, n_freq), out_s...]
where the time goes in v2:
time: 23.5 us; the launch traced here: 23.4 us
  Pallas kernels  21.8 us (93%)
  local copies, waits for them, and re-layouts  1.57 us (7%)
    pallas_call x1, Pallas kernels, body(): pl.pallas_call(functools.partial(kernel, n_support, n_row, n_freq), out_s...  21.8 us
    unnamed x1, local copies, waits for them, and re-layouts  1.57 us

profile of v2, /device:TPU:1, one launch (start us, length us, event | category | flops | bytes accessed | tf_op | source)
XLA Modules:
  0.0 23.4 jit_solution(13642730872097427476)
XLA Ops:
  0.0 21.8 %shard_map.64 = f32[64,512]{1,0:T(8,128)} custom-call(bf16[1,512,2048]{2,1,0:T(8,128)(2,1)} %coh_in.1, s32[32,512]{1,0:T(8,128)} %bitcast.7, bf16[512,2048]{1,0:T(8,128)(2,1)} %infl_in.1, f32[1,2048]{1,0:T(1,128)} %bitcast.8, f32[1,2048]{1,0:T(1,128)} %bitcast.9, bf16[2048,512]{1,0:T(8,128)(2,1)} %shp_in.1), custom_call_target="tpu_custom_call" | custom-call | tf_op jit(solution)/shard_map/pallas_call | solution.py:240
  21.8 1.6 %copy.8 = f32[8,8,512]{2,1,0:T(8,128)} copy(f32[8,8,512]{2,1,0:T(8,128)} %bitcast.6) | data formatting | bytes 262144

commit v3 on v2

--- a/solution.py
+++ b/solution.py
@@ -45,7 +45,7 @@
     coh_in, ph_in, infl_in, mf_in, dp_in, shp_in,
     out_ref,
     coh, ph, infl, mf, dp, shp,
-    tab, f_send, f_recv, r_send, r_recv, d_send, d_recv,
+    shp_t, tab, f_send, f_recv, r_send, r_recv, d_send, d_recv,
     local_sem, a_out, a_in, b_out, b_in, c_out, c_in, d_out, d_in,
 ):
     blocks = n_support * n_row
@@ -91,7 +91,9 @@
     for k in range(1, n_freq):
         pl.semaphore_signal(barrier, inc=1, device_id=to_freq(k), device_id_type=MESH)
 
-    far_first = [k for k in range(1, blocks) if k >= n_row] + [k for k in range(1, blocks) if k < n_row]
+    straight = [k for k in range(n_row, blocks) if k % n_row == 0]
+    far_first = straight + list(range(1, n_row))
+    far_first += [k for k in range(n_row, blocks) if k % n_row]
     near_first = [k for k in range(1, blocks)]
 
     locals_[0].wait()
@@ -120,7 +122,7 @@
 
     a_copies = {}
     for c in range(PIECES):
-        for k in far + near:
+        for k in far_first:
             a_copies[k, c] = send_piece(tab.at[0], tab.at[k], k, c, a_out, a_in)
 
     locals_[1].wait()
@@ -169,6 +171,10 @@
             f_send[k, pieces[c]] = force_term(spectra, k)
             b_copies[k, c] = send_piece(f_send.at[k], f_recv.at[k], k, c, b_out, b_in)
         forces.append(force_term(spectra, 0).astype(jnp.float32))
+    locals_[5].wait()
+    for b in range(blocks):
+        block = slice(b * dofs, (b + 1) * dofs)
+        shp_t[:, block] = shp[block, :].T
     for c in range(PIECES):
         for k in near_first:
             b_copies[k, c].wait_recv()
@@ -207,10 +213,9 @@
     def slab_term(k):
         block_rows = pl.ds(pl.multiple_of(block_to(k) * dofs, dofs), dofs)
         return lax.dot_general(
-            modal, shp[block_rows, :], NT, preferred_element_type=jnp.float32
+            modal, shp_t[:, block_rows], NN, preferred_element_type=jnp.float32
         ).astype(jnp.bfloat16)
 
-    locals_[5].wait()
     d_copies = {}
     for k in far_first:
         d_send[k] = slab_term(k)
@@ -249,6 +254,7 @@
             pltpu.VMEM((1, mode_total), f32),
             pltpu.VMEM((1, mode_total), f32),
             pltpu.VMEM(shapes.shape, bf16),
+            pltpu.VMEM((shapes.shape[1], shapes.shape[0]), bf16),
             pltpu.VMEM((blocks, 2 * real, depth), bf16),
             pltpu.VMEM((blocks, 2 * real, modes), bf16),
             pltpu.VMEM((blocks, 2 * real, modes), bf16),

time: 23.5 us -> 23.4 us (level)
  no operation moved by 1% of the time
where the time goes in v3:
time: 23.4 us; the launch traced here: 23.2 us
  Pallas kernels  21.6 us (92%)
  local copies, waits for them, and re-layouts  1.57 us (7%)
    pallas_call x1, Pallas kernels, body(): pl.pallas_call(functools.partial(kernel, n_support, n_row, n_freq), out_s...  21.6 us
    unnamed x1, local copies, waits for them, and re-layouts  1.57 us

profile of v3, /device:TPU:1, one launch (start us, length us, event | category | flops | bytes accessed | tf_op | source)
XLA Modules:
  0.0 23.2 jit_solution(17825308655087249230)
XLA Ops:
  0.0 21.6 %shard_map.64 = f32[64,512]{1,0:T(8,128)} custom-call(bf16[1,512,2048]{2,1,0:T(8,128)(2,1)} %coh_in.1, s32[32,512]{1,0:T(8,128)} %bitcast.7, bf16[512,2048]{1,0:T(8,128)(2,1)} %infl_in.1, f32[1,2048]{1,0:T(1,128)} %bitcast.8, f32[1,2048]{1,0:T(1,128)} %bitcast.9, bf16[2048,512]{1,0:T(8,128)(2,1)} %shp_in.1), custom_call_target="tpu_custom_call" | custom-call | tf_op jit(solution)/shard_map/pallas_call | solution.py:245
  21.6 1.6 %copy.8 = f32[8,8,512]{2,1,0:T(8,128)} copy(f32[8,8,512]{2,1,0:T(8,128)} %bitcast.6) | data formatting | bytes 262144

commit v4 on v3

--- a/solution.py
+++ b/solution.py
@@ -175,15 +175,18 @@
     for b in range(blocks):
         block = slice(b * dofs, (b + 1) * dofs)
         shp_t[:, block] = shp[block, :].T
-    for c in range(PIECES):
+    def arrived(c):
+        total = forces[c]
         for k in near_first:
             b_copies[k, c].wait_recv()
-            forces[c] += f_recv[k, pieces[c]].astype(jnp.float32)
-    forces = jnp.concatenate(forces, 0)
-
-    force_re, force_im = forces[:real], forces[real:]
-    resp_re = recep_re * force_re - recep_im * force_im
-    resp_im = recep_re * force_im + recep_im * force_re
+            total += f_recv[k, pieces[c]].astype(jnp.float32)
+        return total
+
+    force_re = arrived(0)
+    from_re, turned_re = recep_re * force_re, recep_im * force_re
+    force_im = arrived(1)
+    resp_re = from_re - recep_im * force_im
+    resp_im = recep_re * force_im + turned_re
     for f in range(n_freq):
         rows = slice(f * real_local, (f + 1) * real_local)
         r_send[f] = jnp.concatenate([resp_re[rows], resp_im[rows]], 0).astype(jnp.bfloat16)

time: 23.4 us -> 23.4 us (level)
  no operation moved by 1% of the time
where the time goes in v4:
time: 23.4 us; the launch traced here: 23.2 us
  Pallas kernels  21.6 us (92%)
  local copies, waits for them, and re-layouts  1.57 us (7%)
    pallas_call x1, Pallas kernels, body(): pl.pallas_call(functools.partial(kernel, n_support, n_row, n_freq), out_s...  21.6 us
    unnamed x1, local copies, waits for them, and re-layouts  1.57 us

profile of v4, /device:TPU:1, one launch (start us, length us, event | category | flops | bytes accessed | tf_op | source)
XLA Modules:
  0.0 23.2 jit_solution(17802871790223373350)
XLA Ops:
  0.0 21.6 %shard_map.64 = f32[64,512]{1,0:T(8,128)} custom-call(bf16[1,512,2048]{2,1,0:T(8,128)(2,1)} %coh_in.1, s32[32,512]{1,0:T(8,128)} %bitcast.7, bf16[512,2048]{1,0:T(8,128)(2,1)} %infl_in.1, f32[1,2048]{1,0:T(1,128)} %bitcast.8, f32[1,2048]{1,0:T(1,128)} %bitcast.9, bf16[2048,512]{1,0:T(8,128)(2,1)} %shp_in.1), custom_call_target="tpu_custom_call" | custom-call | tf_op jit(solution)/shard_map/pallas_call | solution.py:248
  21.6 1.6 %copy.8 = f32[8,8,512]{2,1,0:T(8,128)} copy(f32[8,8,512]{2,1,0:T(8,128)} %bitcast.6) | data formatting | bytes 262144
